TPU v7x, 32 devices: a whole 2x2x4 slice. The times are simulated.
32 devices in a mesh: ctx: 4 (over y, x), head: 8 (over z, core).
Axes of the slice: x: 2, y: 2, z: 4, core: 2. Of those that a mesh axis runs over, the one named last changes fastest.
Arguments:
- latent: bfloat16 [1024, 576], P('ctx'), may hold values from -6 to 6
- queries: bfloat16 [1024, 24576], P('ctx', 'head'), may hold values from -300 to 300
- up_weight: bfloat16 [512, 32768], P(None, 'head'), may hold values from -0.25 to 0.25
- out_grad: bfloat16 [1024, 16384], P('ctx', 'head'), may hold values from -6 to 6
- logratio: float32 [1024], P('ctx'), may hold values from -1.5 to 1.5
- student_logprob: float32 [1024], P('ctx'), may hold values from -4 to -0.05
- teacher_logprob: float32 [1024], P('ctx'), may hold values from -4 to -0.05
- group_order: int32 [8], replicated, may hold values from 0 to 7, each once
Outputs:
- attn_output: bfloat16 [1024, 16384], P('ctx', 'head')
- query_grad: bfloat16 [1024, 24576], P('ctx', 'head')
- latent_grad: float32 [1024, 576], P(('ctx', 'head'))
- weight_grad: float32 [512, 32768], P('ctx', 'head')
Inputs may be any that keep to these rules, and one draw needn't show every extreme that they name: Row r of the sequence arrays stands at position group_order[r // 128] * 128 + r % 128 of the rollout.
All inputs are finite; a program needn't handle non-finite values.
Results may differ from a plain program's by a relative error of at most 0.035.
Values may be sent and summed in bfloat16 or wider, within the bound.
A program may use at most 64 MiB of HBM per device.

v0:
```python
import jax
import jax.numpy as jnp
from jax import lax
from jax.sharding import PartitionSpec as P

NOPE = 128
VDIM = 128
KV_RANK = 512
QK = 192


def contract_last(former, latter):
    return lax.dot_general(
        former, latter, (((1,), (1,)), ((), ())), preferred_element_type=jnp.float32
    )


def contract_first(former, latter):
    return lax.dot_general(
        former, latter, (((0,), (0,)), ((), ())), preferred_element_type=jnp.float32
    )


def positions_of(group_order, row_count, group_len):
    row_index = jnp.arange(row_count, dtype=jnp.int32)
    group_slot = row_index // group_len
    onehot = group_slot[:, None] == jnp.arange(group_order.shape[0], dtype=jnp.int32)[None, :]
    starts = jnp.sum(jnp.where(onehot, group_order[None, :], 0), axis=1)
    return starts * group_len + row_index % group_len


def token_weight(logratio, student_logprob, teacher_logprob):
    return jnp.clip(jnp.exp(logratio), 0.8, 1.25) * (teacher_logprob - student_logprob)


def local(
    latent, queries, up_weight, out_grad, logratio, student_logprob, teacher_logprob, group_order
):
    local_rows = latent.shape[0]
    gathered = lax.all_gather(latent, "ctx", axis=0, tiled=True)
    all_rows = gathered.shape[0]
    positions = positions_of(group_order, all_rows, local_rows // 2)
    own_pos = lax.dynamic_slice_in_dim(positions, lax.axis_index("ctx") * local_rows, local_rows)
    visible = positions[None, :] <= own_pos[:, None]
    tok_weight = token_weight(logratio, student_logprob, teacher_logprob)
    head_count = queries.shape[1] // QK
    q_heads = queries.reshape(local_rows, head_count, QK).transpose(1, 0, 2)
    g_heads = out_grad.reshape(local_rows, head_count, VDIM).transpose(1, 0, 2)
    w_heads = up_weight.reshape(KV_RANK, head_count, NOPE + VDIM).transpose(1, 0, 2)
    latent_main = gathered[:, :KV_RANK]
    latent_rope = gathered[:, KV_RANK:]
    logit_scale = QK ** (-0.5)

    def head_step(running, sliced):
        head_query, head_grad, head_weight = sliced
        key_value = jnp.dot(latent_main, head_weight, preferred_element_type=jnp.float32).astype(
            jnp.bfloat16
        )
        key_matrix = jnp.concatenate([key_value[:, :NOPE], latent_rope], axis=1)
        value_matrix = key_value[:, NOPE:]
        score_matrix = contract_last(head_query, key_matrix) * logit_scale
        score_matrix = jnp.where(visible, score_matrix, -jnp.inf)
        row_max = jnp.max(score_matrix, axis=1, keepdims=True)
        numerator = jnp.exp(score_matrix - row_max)
        attn_prob = numerator / jnp.sum(numerator, axis=1, keepdims=True)
        probability_lowered = attn_prob.astype(jnp.bfloat16)
        attention_result = jnp.dot(
            probability_lowered, value_matrix, preferred_element_type=jnp.float32
        )
        output_gradient = (tok_weight[:, None] * head_grad.astype(jnp.float32)).astype(jnp.bfloat16)
        probability_gradient = contract_last(output_gradient, value_matrix)
        row_delta = jnp.sum(
            output_gradient.astype(jnp.float32) * attention_result, axis=1, keepdims=True
        )
        score_gradient = (attn_prob * (probability_gradient - row_delta) * logit_scale).astype(
            jnp.bfloat16
        )
        query_gradient = jnp.dot(score_gradient, key_matrix, preferred_element_type=jnp.float32)
        key_gradient = contract_first(score_gradient, head_query)
        value_gradient = contract_first(probability_lowered, output_gradient)
        grad_kv = jnp.concatenate([key_gradient[:, :NOPE], value_gradient], axis=1).astype(
            jnp.bfloat16
        )
        grad_main = contract_last(grad_kv, head_weight)
        running = running + jnp.concatenate([grad_main, key_gradient[:, NOPE:]], axis=1)
        grad_weight = contract_first(latent_main, grad_kv)
        return (
            running,
            (
                attention_result.astype(jnp.bfloat16),
                query_gradient.astype(jnp.bfloat16),
                grad_weight,
            ),
        )

    start_value = jnp.zeros((all_rows, gathered.shape[1]), jnp.float32)
    latent_terms, stacked = lax.scan(head_step, start_value, (q_heads, g_heads, w_heads))
    attn_output = stacked[0].transpose(1, 0, 2).reshape(local_rows, head_count * VDIM)
    query_grad = stacked[1].transpose(1, 0, 2).reshape(local_rows, head_count * QK)
    weight_terms = stacked[2].transpose(1, 0, 2).reshape(KV_RANK, head_count * (NOPE + VDIM))
    latent_grad = lax.psum_scatter(latent_terms, ("ctx", "head"), scatter_dimension=0, tiled=True)
    weight_grad = lax.psum_scatter(weight_terms, "ctx", scatter_dimension=0, tiled=True)
    return (attn_output, query_grad, latent_grad, weight_grad)


def solution(mesh):
    placed = (
        P("ctx", None),
        P("ctx", "head"),
        P(None, "head"),
        P("ctx", "head"),
        P("ctx"),
        P("ctx"),
        P("ctx"),
        P(),
    )
    return jax.shard_map(
        local,
        mesh=mesh,
        in_specs=placed,
        out_specs=(P("ctx", "head"), P("ctx", "head"), P(("ctx", "head"), None), P("ctx", "head")),
        check_vma=False,
    )
```

profile of v0, /device:TPU:0, one launch (start us, length us, event | category | flops | bytes accessed | tf_op | source)
XLA Modules:
  0.0 487.3 jit_solution(7305015728208449588)
XLA Ops:
  8.0 2.3 copy.30
  10.3 2.6 copy.28
  12.8 6.5 %copy.29 = bf16[512,4096]{0,1:T(8,128)(2,1)} copy(bf16[512,4096]{1,0:T(8,128)(2,1)} %param.12) | data formatting | bytes 8388608 | tf_op args[2]
  19.6 20.6 %all-gather.2.cloned.1.call-done = bf16[1024,576]{0,1:T(8,128)(2,1)} async-done(((bf16[256,576]{0,1:T(8,128)(2,1)}), bf16[1024,576]{0,1:T(8,128)(2,1)}) %all-gather.2.cloned.1.call-update) | async-done | bytes 1179664 | tf_op jit(solution)/shard_map/all_gather | solution.py:40
  40.1 2.3 slice.29
  42.4 1.5 copy.33
  44.0 209.8 %while.17 = (s32[]{:T(128)}, f32[1024,576]{0,1:T(8,128)S(1)}, bf16[16,256,128]{1,2,0:T(8,128)(2,1)}, bf16[16,256,192]{1,2,0:T(8,128)(2,1)}, f32[16,512,256]{1,2,...) while((s32[]{:T(128)}, f32[1024,576]{0,1:T(8,128)S(1)}, ...), condition=%wide.region_5.6_spmd.clone, body=%wide.region_1.5_spmd.clone.sunk | while | flops 1318599936 | bytes 27442372 | solution.py:97
  44.0 1.4 fusion.84
  53.6 1.4 fusion.90
  57.1 1.4 fusion.84
  66.7 1.4 fusion.90
  70.2 1.4 fusion.84
  71.6 1.3 fusion.85
  79.8 1.4 fusion.90
  83.3 1.4 fusion.84
  84.7 1.3 fusion.85
  92.9 1.4 fusion.90
  96.4 1.4 fusion.84
  106.0 1.4 fusion.90
  109.5 1.4 fusion.84
  119.1 1.4 fusion.90
  122.6 1.4 fusion.84
  132.3 1.4 fusion.90
  135.7 1.4 fusion.84
  137.2 1.3 fusion.85
  145.4 1.4 fusion.90
  148.8 1.4 fusion.84
  158.5 1.4 fusion.90
  161.9 1.4 fusion.84
  171.6 1.4 fusion.90
  175.1 1.4 fusion.84
  184.7 1.4 fusion.90
  188.2 1.4 fusion.84
  197.9 1.4 fusion.90
  201.3 1.4 fusion.84
  211.0 1.4 fusion.90
  214.4 1.4 fusion.84
  224.1 1.4 fusion.90
  227.6 1.4 fusion.84
  237.2 1.4 fusion.90
  240.6 1.4 fusion.84
  250.3 1.4 fusion.90
  253.8 2.1 copy.35
  256.0 9.0 %copy.39 = f32[512,4096]{1,0:T(8,128)} copy(f32[512,4096]{0,1:T(8,128)} %bitcast.90) | data formatting | bytes 16777216 | tf_op jit(solution)/shard_map/reshape | solution.py:100
  266.2 1.4 copy.38
  267.6 1.7 copy.37
  269.3 124.6 %reduce-scatter.3.cloned.1.call-done = f32[32,576]{1,0:T(8,128)} async-done(((f32[1024,576]{1,0:T(8,128)}), f32[32,576]{1,0:T(8,128)}) %reduce-scatter.3.cloned.1.call-update) | async-done | bytes 73744 | tf_op jit(solution)/shard_map/reduce_scatter | solution.py:101
  393.9 86.9 %reduce-scatter.5.cloned.1.call-done = f32[128,4096]{1,0:T(8,128)} async-done(((f32[512,4096]{1,0:T(8,128)}), f32[128,4096]{1,0:T(8,128)}) %reduce-scatter.5.cloned.1.call-update) | async-done | bytes 2097168 | tf_op jit(solution)/shard_map/reduce_scatter | solution.py:102
  (250 shorter events, 161.8 us)
Async XLA Ops:
  7.2 33.0 %all-gather.2.cloned.1.call-start = ((), (), s32[]{:S(2)}) async-start(), calls=%async_computation.2 | async-start | bytes 1474560 | tf_op jit(solution)/shard_map/all_gather | solution.py:40
  7.9 386.0 %reduce-scatter.3.cloned.1.call-start = ((), (), s32[]{:S(2)}) async-start(), calls=%async_computation.3 | async-start | bytes 2703360 | tf_op jit(solution)/shard_map/reduce_scatter | solution.py:101
  12.8 6.5 %copy-start.5 = (s32[8]{0:T(128)S(1)}, s32[8]{0:T(128)}, u32[]{:S(2)}) copy-start(s32[8]{0:T(128)} %param.17) | copy-start | bytes 100
  12.8 6.7 %copy-start.2 = (f32[256]{0:T(256)S(1)}, f32[256]{0:T(256)}, u32[]{:S(2)}) copy-start(f32[256]{0:T(256)} %param.16) | copy-start | bytes 3076
  12.8 6.7 %copy-start.3 = (f32[256]{0:T(256)S(1)}, f32[256]{0:T(256)}, u32[]{:S(2)}) copy-start(f32[256]{0:T(256)} %param.15) | copy-start | bytes 3076
  12.8 6.7 %copy-start.4 = (f32[256]{0:T(256)S(1)}, f32[256]{0:T(256)}, u32[]{:S(2)}) copy-start(f32[256]{0:T(256)} %param.14) | copy-start | bytes 3076
  40.1 3.8 slice-start
  255.9 224.8 %reduce-scatter.5.cloned.1.call-start = ((), (), s32[]{:S(2)}) async-start(), calls=%async_computation.4 | async-start | bytes 10485760 | tf_op jit(solution)/shard_map/reduce_scatter | solution.py:102
  264.9 1.2 copy-start.1
  265.0 2.6 copy-start
Sparse Core Ops, SparseCore 0:
  9.8 30.2 all-gather.1
  256.0 137.8 reduce-scatter.2
  397.5 83.1 reduce-scatter.4
where the time goes:
time: 492 us; the launch traced here: 487 us
  waiting for transfers between devices  233 us (47%)
  matrix products  175 us (36%)
  local copies, waits for them, and re-layouts  41.9 us (9%)
  other arithmetic  22.4 us (5%)
  between operations  13.8 us (3%)
    reduce_scatter x1, waiting for transfers between devices, local(): lax.psum_scatter(latent_terms, ('ctx', 'head'), scatter_dimension=0, tile...  125 us
    reduce_scatter x1, waiting for transfers between devices, local(): lax.psum_scatter(weight_terms, 'ctx', scatter_dimension=0, tiled=True)  86.9 us
    dot_general x48, matrix products, contract_last(): lax.dot_general(former, latter, (((1,), (1,)), ((), ())), preferred_eleme...  62 us
    dot_general x48, matrix products, contract_first(): lax.dot_general(former, latter, (((0,), (0,)), ((), ())), preferred_eleme...  55.8 us
    dot_general x16, matrix products, head_step(): jnp.dot(latent_main, head_weight, preferred_element_type=jnp.float32)  22.6 us
    all_gather x1, waiting for transfers between devices, local(): gathered = lax.all_gather(latent, 'ctx', axis=0, tiled=True)  20.6 us
    dot_general x16, matrix products, head_step(): jnp.dot(probability_lowered, value_matrix, preferred_element_type=jnp.flo...  18.8 us
    unnamed x17, local copies, waits for them, and re-layouts  15.8 us
  transfers between devices with their start and end apart: 3, of which 3 were waited for; matrix products, arithmetic and copies ran while one was open for 5% of the time, Pallas kernels for 0%

commit v1 on v0

v1 whole, which is shorter than its diff:
```python
import functools

import jax
import jax.numpy as jnp
from jax import lax
from jax.experimental import pallas as pl
from jax.experimental.pallas import tpu as pltpu
from jax.sharding import PartitionSpec as P

NOPE = 128
VDIM = 128
KV_RANK = 512
QK = 192
ROPE = QK - NOPE
GROUP = 128
HIDDEN = -1e30


def dot(a, b):
    return jnp.dot(a, b, preferred_element_type=jnp.float32)


def dot_last(a, b):
    return lax.dot_general(a, b, (((1,), (1,)), ((), ())), preferred_element_type=jnp.float32)


def fill_bias(order_ref, bias, rows, n_slots):
    own = lax.axis_index("ctx") * (rows // GROUP)
    query_pos = jnp.concatenate(
        [
            order_ref[own + s] * GROUP + lax.broadcasted_iota(jnp.int32, (GROUP, GROUP), 1)
            for s in range(rows // GROUP)
        ],
        axis=1,
    )

    def slot(s, carry):
        key_pos = order_ref[s] * GROUP + lax.broadcasted_iota(jnp.int32, (GROUP, rows), 0)
        start = pl.multiple_of(s * GROUP, GROUP)
        bias[pl.ds(start, GROUP), :] = jnp.where(key_pos <= query_pos, 0.0, HIDDEN)
        return carry

    lax.fori_loop(0, n_slots, slot, 0)


def head_pair(pair, rope, q_ref, kv, dout, attn_ref, qg_ref, rope_acc, bias):
    scale = QK**-0.5
    q_at = pl.multiple_of(pair * (2 * QK), 2 * QK)
    o_at = pl.multiple_of(pair * (2 * VDIM), 2 * VDIM)
    query_pair = q_ref[:, pl.ds(q_at, 2 * QK)]
    query_grads = []
    rope_sum = None
    for j in range(2):
        kv_at = pl.multiple_of(pair * 512 + j * 256, 256)
        v_at = pl.multiple_of(pair * 256 + j * VDIM, VDIM)
        key = jnp.concatenate([kv[:, pl.ds(kv_at, NOPE)], rope], axis=1)
        value = kv[:, pl.ds(kv_at + NOPE, VDIM)]
        query = query_pair[:, j * QK : (j + 1) * QK]
        grad = dout[:, pl.ds(v_at, VDIM)]
        score = dot_last(key, query) + bias[...]
        top = jnp.max(score, axis=0, keepdims=True)
        weight = jnp.exp((score - top) * scale)
        prob = weight * (1.0 / jnp.sum(weight, axis=0, keepdims=True))
        prob_low = prob.astype(jnp.bfloat16)
        out_t = dot(value.T, prob_low)
        delta = jnp.sum(grad.astype(jnp.float32).T * out_t, axis=0, keepdims=True)
        attn_ref[:, pl.ds(v_at, VDIM)] = out_t.T.astype(jnp.bfloat16)
        dprob = dot_last(value, grad)
        dscore = (prob * (dprob - delta) * scale).astype(jnp.bfloat16)
        query_grads.append(dot(key.T, dscore).T)
        dkey = dot(dscore, query)
        dvalue = dot(prob_low, grad)
        kv[:, pl.ds(kv_at, NOPE)] = dkey[:, :NOPE].astype(jnp.bfloat16)
        kv[:, pl.ds(kv_at + NOPE, VDIM)] = dvalue.astype(jnp.bfloat16)
        part = dkey[:, NOPE:]
        rope_sum = part if rope_sum is None else rope_sum + part
    qg_ref[:, pl.ds(q_at, 2 * QK)] = jnp.concatenate(query_grads, axis=1).astype(jnp.bfloat16)
    rope_acc[...] += rope_sum


def kernel(
    lat_ref, q_ref, w_ref, g_ref, lr_ref, sl_ref, tl_ref, order_ref,
    attn_ref, qg_ref, lt_ref, wt_ref,
    kv, dout, bias, lat_t, rope_acc,
):
    rows, keys = q_ref.shape[0], lat_ref.shape[0]
    n_pairs = q_ref.shape[1] // (2 * QK)
    fill_bias(order_ref, bias, rows, keys // GROUP)
    tok_weight = jnp.clip(jnp.exp(lr_ref[...]), 0.8, 1.25) * (tl_ref[...] - sl_ref[...])
    tok_weight = jnp.broadcast_to(tok_weight, (128, rows)).T
    lat_t[...] = lat_ref[:, :KV_RANK].T
    rope_acc[...] = jnp.zeros_like(rope_acc)

    def pair_step(pair, carry):
        at = pl.multiple_of(pair * 512, 512)
        o_at = pl.multiple_of(pair * 256, 256)
        two = jnp.concatenate([tok_weight, tok_weight], axis=1)
        dout[:, pl.ds(o_at, 256)] = (two * g_ref[:, pl.ds(o_at, 256)].astype(jnp.float32)).astype(
            jnp.bfloat16
        )
        kv[:, pl.ds(at, 512)] = dot(lat_ref[:, :KV_RANK], w_ref[:, pl.ds(at, 512)]).astype(
            jnp.bfloat16
        )
        head_pair(
            pair, lat_ref[:, KV_RANK:], q_ref, kv, dout, attn_ref, qg_ref, rope_acc, bias
        )
        wt_ref[:, pl.ds(at, 512)] = dot(lat_t[...], kv[:, pl.ds(at, 512)]).astype(jnp.bfloat16)
        return carry

    lax.fori_loop(0, n_pairs, pair_step, 0)

    def chunk(i, carry):
        at = pl.multiple_of(i * 256, 256)
        lt_ref[pl.ds(at, 256), :KV_RANK] = dot_last(kv[pl.ds(at, 256), :], w_ref[...]).astype(
            jnp.bfloat16
        )
        lt_ref[pl.ds(at, 256), KV_RANK:] = rope_acc[pl.ds(at, 256), :].astype(jnp.bfloat16)
        return carry

    lax.fori_loop(0, keys // 256, chunk, 0)


def local(
    latent, queries, up_weight, out_grad, logratio, student_logprob, teacher_logprob, group_order
):
    gathered = lax.all_gather(latent, "ctx", axis=0, tiled=True)
    rows, keys = latent.shape[0], gathered.shape[0]
    vmem = pl.BlockSpec(memory_space=pltpu.VMEM)
    smem = pl.BlockSpec(memory_space=pltpu.SMEM)
    bf16 = jnp.bfloat16
    attn, query_grad, latent_terms, weight_terms = pl.pallas_call(
        kernel,
        out_shape=(
            jax.ShapeDtypeStruct(out_grad.shape, bf16),
            jax.ShapeDtypeStruct(queries.shape, bf16),
            jax.ShapeDtypeStruct(gathered.shape, bf16),
            jax.ShapeDtypeStruct(up_weight.shape, bf16),
        ),
        in_specs=[vmem] * 7 + [smem],
        out_specs=[vmem] * 4,
        scratch_shapes=[
            pltpu.VMEM((keys, up_weight.shape[1]), bf16),
            pltpu.VMEM((rows, out_grad.shape[1]), bf16),
            pltpu.VMEM((keys, rows), jnp.float32),
            pltpu.VMEM((KV_RANK, keys), bf16),
            pltpu.VMEM((keys, ROPE), jnp.float32),
        ],
        compiler_params=pltpu.CompilerParams(vmem_limit_bytes=60 * 2**20),
    )(
        gathered,
        queries,
        up_weight,
        out_grad,
        logratio.reshape(1, rows),
        student_logprob.reshape(1, rows),
        teacher_logprob.reshape(1, rows),
        group_order,
    )
    latent_grad = lax.psum_scatter(latent_terms, ("ctx", "head"), scatter_dimension=0, tiled=True)
    weight_grad = lax.psum_scatter(weight_terms, "ctx", scatter_dimension=0, tiled=True)
    return (
        attn,
        query_grad,
        latent_grad.astype(jnp.float32),
        weight_grad.astype(jnp.float32),
    )


def solution(mesh):
    placed = (
        P("ctx", None),
        P("ctx", "head"),
        P(None, "head"),
        P("ctx", "head"),
        P("ctx"),
        P("ctx"),
        P("ctx"),
        P(),
    )
    return jax.shard_map(
        local,
        mesh=mesh,
        in_specs=placed,
        out_specs=(P("ctx", "head"), P("ctx", "head"), P(("ctx", "head"), None), P("ctx", "head")),
        check_vma=False,
    )
```

time: 492 us -> 288 us (0.59)
  matrix products: 175 us -> 0 us
  Pallas kernels: 0 us -> 49.1 us
  local copies, waits for them, and re-layouts: 41.9 us -> 1.86 us
  other arithmetic: 22.4 us -> 4.17 us
  waiting for transfers between devices: 233 us -> 219 us
    dot_general x144 -> x0, matrix products: 175 us -> none  [the longest x48 62 us: contract_last(): lax.dot_general(former, latter, (((1,), (1,)), ((), ())), preferred_eleme...]
    pallas_call x0 -> x1, Pallas kernels: none -> 49.1 us  [local(): pl.pallas_call(kernel, out_shape=(jax.ShapeDtypeStruct(out_grad.shape, bf...]
    reduce_scatter x1, waiting for transfers between devices: 86.9 us -> 51.1 us  [local(): lax.psum_scatter(weight_terms, 'ctx', scatter_dimension=0, tiled=True)]
    unnamed x17 -> x1, local copies, waits for them, and re-layouts: 15.8 us -> 1.86 us
    add x17 -> x0, other arithmetic: 13 us -> none  [the longest x16 13 us: head_step(): running + jnp.concatenate([grad_main, key_gradient[:, NOPE:]], axis=1)]
    all_gather x1, waiting for transfers between devices: 20.6 us -> 32.8 us  [local(): gathered = lax.all_gather(latent, 'ctx', axis=0, tiled=True)]
    reshape x2 -> x0, local copies, waits for them, and re-layouts: 10.4 us -> none  [the longest x1 8.99 us: local(): stacked[2].transpose(1, 0, 2).reshape(KV_RANK, head_count * (NOPE + VDIM))]
    dynamic_update_slice x16 -> x0, local copies, waits for them, and re-layouts: 10.1 us -> none  [local(): lax.scan(head_step, start_value, (q_heads, g_heads, w_heads))]
  transfers between devices with their start and end apart: 3 -> 3, of which waited for: 3 -> 3; matrix products, arithmetic and copies ran while one was open for 5% -> 0% of each run, Pallas kernels for 0% -> 0%
where the time goes in v1:
time: 288 us
  waiting for transfers between devices  219 us (76%)
  Pallas kernels  49.1 us (17%)
  between operations  13.7 us (5%)
  other arithmetic  4.17 us (1%)
    reduce_scatter x1, waiting for transfers between devices, local(): lax.psum_scatter(latent_terms, ('ctx', 'head'), scatter_dimension=0, tile...  135 us
    reduce_scatter x1, waiting for transfers between devices, local(): lax.psum_scatter(weight_terms, 'ctx', scatter_dimension=0, tiled=True)  51.1 us
    pallas_call x1, Pallas kernels, local(): pl.pallas_call(kernel, out_shape=(jax.ShapeDtypeStruct(out_grad.shape, bf...  49.1 us
    all_gather x1, waiting for transfers between devices, local(): gathered = lax.all_gather(latent, 'ctx', axis=0, tiled=True)  32.8 us
  transfers between devices with their start and end apart: 3, of which 3 were waited for; matrix products, arithmetic and copies ran while one was open for 0% of the time, Pallas kernels for 0%

profile of v1, /device:TPU:0, one launch (start us, length us, event | category | flops | bytes accessed | tf_op | source)
XLA Modules:
  0.0 288.2 jit_solution(16955817053988238205)
XLA Ops:
  7.2 0.0 all-gather.2.cloned.1.call-start
  7.2 1.9 copy.12
  9.1 0.0 all-gather.2.cloned.1.call-update
  9.1 0.0 reduce-scatter.3.cloned.1.call-start
  9.1 32.8 %all-gather.2.cloned.1.call-done.lat_ref = bf16[1024,576]{1,0:T(8,128)(2,1)} async-done(((bf16[256,576]{1,0:T(8,128)(2,1)}), bf16[1024,576]{1,0:T(8,128)(2,1)}) %all-gather.2.cloned.1.call-update) | async-done | bytes 1179664 | tf_op jit(solution)/shard_map/all_gather | solution.py:126
  42.0 49.1 %shard_map.111 = (bf16[256,2048]{1,0:T(8,128)(2,1)}, bf16[256,3072]{1,0:T(8,128)(2,1)}, bf16[1024,576]{1,0:T(8,128)(2,1)}, bf16[512,4096]{1,0:T(8,128)(2,1)}) custom-call(bf16[1024,576]{1,0:T(8,128)(2,1)} %all-gather.2.cloned.1.call-done.lat_ref, bf16[256,3072]{1,0:T(8,128)(2,1)} %q_ref.1, bf16[512,4096]{1,0:T(8,128)(2,1)} %w_ref.1, ...), custom_call_target="tpu_custom_call" | custom-call | tf_op jit(solution)/shard_map/pallas_call | solution.py:131
  91.0 0.0 reduce-scatter.3.cloned.1.call-update
  91.0 0.0 reduce-scatter.5.cloned.1.call-start
  91.1 0.7 reduce-scatter.5.cloned.1.call-update
  91.8 134.6 %reduce-scatter.3.cloned.1.call-done = bf16[32,576]{1,0:T(8,128)(2,1)} async-done(((bf16[1024,576]{1,0:T(8,128)(2,1)}), bf16[32,576]{1,0:T(8,128)(2,1)}) %reduce-scatter.3.cloned.1.call-update) | async-done | bytes 36880 | tf_op jit(solution)/shard_map/reduce_scatter | solution.py:159
  226.4 1.4 convert_element_type.6
  227.8 51.1 %reduce-scatter.5.cloned.1.call-done = bf16[128,4096]{1,0:T(8,128)(2,1)} async-done(((bf16[512,4096]{1,0:T(8,128)(2,1)}), bf16[128,4096]{1,0:T(8,128)(2,1)}) %reduce-scatter.5.cloned.1.call-update) | async-done | bytes 1048592 | tf_op jit(solution)/shard_map/reduce_scatter | solution.py:160
  278.9 2.8 convert_element_type.7
Async XLA Ops:
  7.2 34.8 %all-gather.2.cloned.1.call-start = ((), (), s32[]{:S(2)}) async-start(), calls=%async_computation.2 | async-start | bytes 1638400 | tf_op jit(solution)/shard_map/all_gather | solution.py:126
  9.1 217.3 %reduce-scatter.3.cloned.1.call-start = ((), (), s32[]{:S(2)}) async-start(), calls=%async_computation.3 | async-start | bytes 1351680 | tf_op jit(solution)/shard_map/reduce_scatter | solution.py:159
  91.0 187.8 %reduce-scatter.5.cloned.1.call-start = ((), (), s32[]{:S(2)}) async-start(), calls=%async_computation.4 | async-start | bytes 5242880 | tf_op jit(solution)/shard_map/reduce_scatter | solution.py:160
Sparse Core Ops, SparseCore 0:
  10.4 31.4 all-gather.1
  91.2 135.1 reduce-scatter.2
  229.6 49.2 reduce-scatter.4

commit v2 on v1

--- a/solution.py
+++ b/solution.py
@@ -78,91 +78,272 @@
     rope_acc[...] += rope_sum
 
 
+def remote(src, dst, send_sem, recv_sem, ctx, head):
+    return pltpu.make_async_remote_copy(
+        src_ref=src,
+        dst_ref=dst,
+        send_sem=send_sem,
+        recv_sem=recv_sem,
+        device_id=(ctx, head),
+        device_id_type=pl.DeviceIdType.MESH,
+    )
+
+
 def kernel(
-    lat_ref, q_ref, w_ref, g_ref, lr_ref, sl_ref, tl_ref, order_ref,
-    attn_ref, qg_ref, lt_ref, wt_ref,
-    kv, dout, bias, lat_t, rope_acc,
+    n_ctx, n_head,
+    lat_ref, lr_ref, sl_ref, tl_ref, order_ref, q_hbm, w_hbm, g_hbm,
+    attn_ref, qg_ref, lg_ref, wg_ref,
+    lat, q_ref, w_ref, g_ref, kv, dout, bias, lat_t, rope_acc,
+    wt, wt_in, terms, core_in, comb, ctx_in, zsum, z_in,
+    load_sem, lat_send, lat_recv, fwd_send, fwd_recv, wt_send, wt_recv,
+    core_send, core_recv, ctx_send, ctx_recv, z_send, z_recv,
 ):
-    rows, keys = q_ref.shape[0], lat_ref.shape[0]
+    rows, keys = lat_ref.shape[0], lat.shape[0]
     n_pairs = q_ref.shape[1] // (2 * QK)
+    n_z = n_head // 2
+    half = rows // 2
+    own_rows = KV_RANK // n_ctx
+    f32, bf16 = jnp.float32, jnp.bfloat16
+    me, head = lax.axis_index("ctx"), lax.axis_index("head")
+    core, z = head % 2, head // 2
+    partner = head + 1 - 2 * core
+
+    loads = [
+        pltpu.make_async_copy(src, dst, load_sem.at[i])
+        for i, (src, dst) in enumerate(((g_hbm, g_ref), (w_hbm, w_ref), (q_hbm, q_ref)))
+    ]
+    for load in loads:
+        load.start()
+
+    def ctx_peer(d):
+        return (me + d) % n_ctx
+
+    def ctx_source(d):
+        return (me + n_ctx - d) % n_ctx
+
+    def z_peer(d):
+        return (z + d) % n_z
+
+    barrier = pltpu.get_barrier_semaphore()
+    peers = [(ctx_peer(d), head) for d in range(1, n_ctx)]
+    peers += [(me, z_peer(d) * 2 + core) for d in range(1, n_z)]
+    peers += [(me, partner)]
+    for peer in peers:
+        pl.semaphore_signal(barrier, inc=1, device_id=peer, device_id_type=pl.DeviceIdType.MESH)
+    pl.semaphore_wait(barrier, len(peers))
+
+    def lat_rows(block, part):
+        return lat.at[pl.ds(pl.multiple_of(block * rows + part * half, half), half), :]
+
+    def lat_copy(d, to, block, part):
+        return remote(
+            lat_ref.at[pl.ds(pl.multiple_of(core * half, half), half), :],
+            lat_rows(block, part), lat_send.at[d - 1], lat_recv.at[d - 1], to, head,
+        )
+
+    def fwd_copy(d, part):
+        place = lat_rows(ctx_source(d), part)
+        return remote(place, place, fwd_send.at[d - 1], fwd_recv.at[d - 1], me, partner)
+
+    order = [2, 1, 3] if n_ctx == 4 else list(range(1, n_ctx))
+    for d in order:
+        lat_copy(d, ctx_peer(d), me, core).start()
+    lat[pl.ds(pl.multiple_of(me * rows, rows), rows), :] = lat_ref[...]
+
     fill_bias(order_ref, bias, rows, keys // GROUP)
     tok_weight = jnp.clip(jnp.exp(lr_ref[...]), 0.8, 1.25) * (tl_ref[...] - sl_ref[...])
     tok_weight = jnp.broadcast_to(tok_weight, (128, rows)).T
-    lat_t[...] = lat_ref[:, :KV_RANK].T
+    two = jnp.concatenate([tok_weight, tok_weight], axis=1)
     rope_acc[...] = jnp.zeros_like(rope_acc)
+    loads[0].wait()
+
+    def weigh(pair, carry):
+        at = pl.ds(pl.multiple_of(pair * 256, 256), 256)
+        dout[:, at] = (two * g_ref[:, at].astype(f32)).astype(bf16)
+        return carry
+
+    lax.fori_loop(0, n_pairs, weigh, 0)
+
+    for d in order:
+        lat_copy(d, ctx_peer(d), ctx_source(d), core).wait_recv()
+        fwd_copy(d, core).start()
+    for d in order:
+        fwd_copy(d, 1 - core).wait_recv()
+    lat_t[...] = lat[:, :KV_RANK].T
+    loads[1].wait()
+    loads[2].wait()
+
+    def wt_copy(d, pair):
+        to = ctx_peer(d)
+        return remote(
+            wt.at[pair, pl.ds(pl.multiple_of(to * own_rows, own_rows), own_rows), :],
+            wt_in.at[d - 1, pair], wt_send.at[d - 1, pair], wt_recv.at[d - 1, pair], to, head,
+        )
 
     def pair_step(pair, carry):
         at = pl.multiple_of(pair * 512, 512)
-        o_at = pl.multiple_of(pair * 256, 256)
-        two = jnp.concatenate([tok_weight, tok_weight], axis=1)
-        dout[:, pl.ds(o_at, 256)] = (two * g_ref[:, pl.ds(o_at, 256)].astype(jnp.float32)).astype(
-            jnp.bfloat16
-        )
-        kv[:, pl.ds(at, 512)] = dot(lat_ref[:, :KV_RANK], w_ref[:, pl.ds(at, 512)]).astype(
-            jnp.bfloat16
-        )
-        head_pair(
-            pair, lat_ref[:, KV_RANK:], q_ref, kv, dout, attn_ref, qg_ref, rope_acc, bias
-        )
-        wt_ref[:, pl.ds(at, 512)] = dot(lat_t[...], kv[:, pl.ds(at, 512)]).astype(jnp.bfloat16)
+        kv[:, pl.ds(at, 512)] = dot(lat[:, :KV_RANK], w_ref[:, pl.ds(at, 512)]).astype(bf16)
+        head_pair(pair, lat[:, KV_RANK:], q_ref, kv, dout, attn_ref, qg_ref, rope_acc, bias)
+        wt[pair] = dot(lat_t[...], kv[:, pl.ds(at, 512)]).astype(bf16)
+        for d in order:
+            wt_copy(d, pair).start()
         return carry
 
     lax.fori_loop(0, n_pairs, pair_step, 0)
 
+    def core_copy(block):
+        return remote(
+            terms.at[block, :, 1 - core], core_in.at[block],
+            core_send.at[block], core_recv.at[block], me, partner,
+        )
+
+    def ctx_copy(d):
+        return remote(
+            comb.at[d], ctx_in.at[d - 1], ctx_send.at[d - 1], ctx_recv.at[d - 1], ctx_peer(d), head
+        )
+
+    def z_copy(d):
+        return remote(
+            zsum.at[z_peer(d)], z_in.at[d - 1], z_send.at[d - 1], z_recv.at[d - 1],
+            me, z_peer(d) * 2 + core,
+        )
+
+    def merged(block):
+        core_copy(block).wait_recv()
+        return terms[block, :, core].astype(f32) + core_in[block].astype(f32)
+
     def chunk(i, carry):
-        at = pl.multiple_of(i * 256, 256)
-        lt_ref[pl.ds(at, 256), :KV_RANK] = dot_last(kv[pl.ds(at, 256), :], w_ref[...]).astype(
-            jnp.bfloat16
-        )
-        lt_ref[pl.ds(at, 256), KV_RANK:] = rope_acc[pl.ds(at, 256), :].astype(jnp.bfloat16)
-        return carry
-
-    lax.fori_loop(0, keys // 256, chunk, 0)
+        block = (me + 1 + i) % n_ctx
+        at = pl.ds(pl.multiple_of(block * rows, rows), rows)
+        main = dot_last(kv[at, :], w_ref[...])
+        whole = jnp.concatenate([main, rope_acc[at, :]], axis=1).astype(bf16)
+        terms[block] = whole.reshape(terms.shape[1:])
+        core_copy(block).start()
+
+        @pl.when(i > 0)
+        def _():
+            comb[i] = merged((me + i) % n_ctx).astype(bf16)
+            ctx_copy(i).start()
+
+        return carry
+
+    lax.fori_loop(0, n_ctx, chunk, 0)
+    total = merged(me)
+    for d in order:
+        ctx_copy(d).wait_recv()
+        total += ctx_in[d - 1].astype(f32)
+    zsum[...] = total.astype(bf16)
+    for d in range(1, n_z):
+        z_copy(d).start()
+
+    def gather_weight(pair, carry):
+        at = pl.ds(pl.multiple_of(pair * 512, 512), 512)
+        mine = pl.ds(pl.multiple_of(me * own_rows, own_rows), own_rows)
+        total = wt[pair, mine, :].astype(f32)
+        for d in order:
+            wt_copy(d, pair).wait_recv()
+            total += wt_in[d - 1, pair].astype(f32)
+        wg_ref[:, at] = total
+        return carry
+
+    lax.fori_loop(0, n_pairs, gather_weight, 0)
+
+    final = zsum[z].astype(f32)
+    for d in range(1, n_z):
+        z_copy(d).wait_recv()
+        final += z_in[d - 1].astype(f32)
+    lg_ref[...] = final
+
+    for d in order:
+        lat_copy(d, ctx_peer(d), me, core).wait_send()
+        fwd_copy(d, core).wait_send()
+        ctx_copy(d).wait_send()
+    for d in range(1, n_z):
+        z_copy(d).wait_send()
+
+    def drain_core(block, carry):
+        core_copy(block).wait_send()
+        return carry
+
+    lax.fori_loop(0, n_ctx, drain_core, 0)
+
+    def drain_weight(pair, carry):
+        for d in order:
+            wt_copy(d, pair).wait_send()
+        return carry
+
+    lax.fori_loop(0, n_pairs, drain_weight, 0)
 
 
 def local(
+    n_ctx, n_head,
     latent, queries, up_weight, out_grad, logratio, student_logprob, teacher_logprob, group_order
 ):
-    gathered = lax.all_gather(latent, "ctx", axis=0, tiled=True)
-    rows, keys = latent.shape[0], gathered.shape[0]
+    rows, width = latent.shape
+    keys = rows * n_ctx
+    n_z, per = n_head // 2, rows // n_head
+    n_pairs = queries.shape[1] // (2 * QK)
+    own_rows = KV_RANK // n_ctx
     vmem = pl.BlockSpec(memory_space=pltpu.VMEM)
     smem = pl.BlockSpec(memory_space=pltpu.SMEM)
-    bf16 = jnp.bfloat16
-    attn, query_grad, latent_terms, weight_terms = pl.pallas_call(
-        kernel,
+    anywhere = pl.BlockSpec(memory_space=pl.ANY)
+    bf16, f32 = jnp.bfloat16, jnp.float32
+    dma = pltpu.SemaphoreType.DMA
+    shape = jax.ShapeDtypeStruct
+    return pl.pallas_call(
+        functools.partial(kernel, n_ctx, n_head),
         out_shape=(
-            jax.ShapeDtypeStruct(out_grad.shape, bf16),
-            jax.ShapeDtypeStruct(queries.shape, bf16),
-            jax.ShapeDtypeStruct(gathered.shape, bf16),
-            jax.ShapeDtypeStruct(up_weight.shape, bf16),
+            shape(out_grad.shape, bf16),
+            shape(queries.shape, bf16),
+            shape((per, width), f32),
+            shape((own_rows, up_weight.shape[1]), f32),
         ),
-        in_specs=[vmem] * 7 + [smem],
+        in_specs=[vmem] * 4 + [smem] + [anywhere] * 3,
         out_specs=[vmem] * 4,
         scratch_shapes=[
+            pltpu.VMEM((keys, width), bf16),
+            pltpu.VMEM(queries.shape, bf16),
+            pltpu.VMEM(up_weight.shape, bf16),
+            pltpu.VMEM(out_grad.shape, bf16),
             pltpu.VMEM((keys, up_weight.shape[1]), bf16),
-            pltpu.VMEM((rows, out_grad.shape[1]), bf16),
-            pltpu.VMEM((keys, rows), jnp.float32),
+            pltpu.VMEM(out_grad.shape, bf16),
+            pltpu.VMEM((keys, rows), f32),
             pltpu.VMEM((KV_RANK, keys), bf16),
-            pltpu.VMEM((keys, ROPE), jnp.float32),
+            pltpu.VMEM((keys, ROPE), f32),
+            pltpu.VMEM((n_pairs, KV_RANK, 512), bf16),
+            pltpu.VMEM((n_ctx - 1, n_pairs, own_rows, 512), bf16),
+            pltpu.VMEM((n_ctx, n_z, 2, per, width), bf16),
+            pltpu.VMEM((n_ctx, n_z, per, width), bf16),
+            pltpu.VMEM((n_ctx, n_z, per, width), bf16),
+            pltpu.VMEM((n_ctx - 1, n_z, per, width), bf16),
+            pltpu.VMEM((n_z, per, width), bf16),
+            pltpu.VMEM((n_z - 1, per, width), bf16),
+            dma((3,)),
+            dma((n_ctx - 1,)),
+            dma((n_ctx - 1,)),
+            dma((n_ctx - 1,)),
+            dma((n_ctx - 1,)),
+            dma((n_ctx - 1, n_pairs)),
+            dma((n_ctx - 1, n_pairs)),
+            dma((n_ctx,)),
+            dma((n_ctx,)),
+            dma((n_ctx - 1,)),
+            dma((n_ctx - 1,)),
+            dma((n_z - 1,)),
+            dma((n_z - 1,)),
         ],
-        compiler_params=pltpu.CompilerParams(vmem_limit_bytes=60 * 2**20),
+        compiler_params=pltpu.CompilerParams(
+            vmem_limit_bytes=60 * 2**20, collective_id=0, has_side_effects=True
+        ),
     )(
-        gathered,
-        queries,
-        up_weight,
-        out_grad,
+        latent,
         logratio.reshape(1, rows),
         student_logprob.reshape(1, rows),
         teacher_logprob.reshape(1, rows),
         group_order,
-    )
-    latent_grad = lax.psum_scatter(latent_terms, ("ctx", "head"), scatter_dimension=0, tiled=True)
-    weight_grad = lax.psum_scatter(weight_terms, "ctx", scatter_dimension=0, tiled=True)
-    return (
-        attn,
-        query_grad,
-        latent_grad.astype(jnp.float32),
-        weight_grad.astype(jnp.float32),
+        queries,
+        up_weight,
+        out_grad,
     )
 
 
@@ -178,7 +359,7 @@
         P(),
     )
     return jax.shard_map(
-        local,
+        functools.partial(local, mesh.shape["ctx"], mesh.shape["head"]),
         mesh=mesh,
         in_specs=placed,
         out_specs=(P("ctx", "head"), P("ctx", "head"), P(("ctx", "head"), None), P("ctx", "head")),

time: 288 us -> 92 us (0.32)
  waiting for transfers between devices: 219 us -> 0 us
  Pallas kernels: 49.1 us -> 83.3 us
  between operations: 13.7 us -> 0.66 us
  local copies, waits for them, and re-layouts: 1.86 us -> 7.8 us
  other arithmetic: 4.17 us -> 0 us
    reduce_scatter x2 -> x0, waiting for transfers between devices: 186 us -> none  [the longest x1 135 us: local(): lax.psum_scatter(latent_terms, ('ctx', 'head'), scatter_dimension=0, tile...]
    pallas_call x1, Pallas kernels: 49.1 us -> 83.3 us  [local(): pl.pallas_call(functools.partial(kernel, n_ctx, n_head), out_shape=(shape...]
    all_gather x1 -> x0, waiting for transfers between devices: 32.8 us -> none  [local(): gathered = lax.all_gather(latent, 'ctx', axis=0, tiled=True)]
    unnamed x1 -> x11, local copies, waits for them, and re-layouts: 1.86 us -> 7.8 us
    convert_element_type x2 -> x0, other arithmetic: 4.17 us -> none  [the longest x1 2.76 us: local(): weight_grad.astype(jnp.float32)]
  transfers between devices with their start and end apart: 3 -> 0, of which waited for: 3 -> 0; matrix products, arithmetic and copies ran while one was open for 0% -> 0% of each run, Pallas kernels for 0% -> 0%
where the time goes in v2:
time: 92 us; the launch traced here: 91.8 us
  Pallas kernels  83.3 us (91%)
  local copies, waits for them, and re-layouts  7.8 us (8%)
    pallas_call x1, Pallas kernels, local(): pl.pallas_call(functools.partial(kernel, n_ctx, n_head), out_shape=(shape...  83.3 us
    unnamed x11, local copies, waits for them, and re-layouts  7.8 us

profile of v2, /device:TPU:0, one launch (start us, length us, event | category | flops | bytes accessed | tf_op | source)
XLA Modules:
  0.0 91.8 jit_solution(13922913283112448664)
XLA Ops:
  0.6 1.9 %copy.12.lat_ref = bf16[256,576]{1,0:T(8,128)(2,1)} copy(bf16[256,576]{0,1:T(8,128)(2,1)} %param.8) | data formatting | bytes 589824 | tf_op args[0]
  2.5 83.3 %shard_map.111 = (bf16[256,2048]{1,0:T(8,128)(2,1)}, bf16[256,3072]{1,0:T(8,128)(2,1)}, f32[32,576]{1,0:T(8,128)}, f32[128,4096]{1,0:T(8,128)}) custom-call(bf16[256,576]{1,0:T(8,128)(2,1)} %copy.12.lat_ref, f32[1,256]{1,0:T(1,128)} %bitcast.3, f32[1,256]{1,0:T(1,128)} %bitcast.4, f32[1,256]{1,0:T(1,128)} %bitcast.5, s32[8]{0:T(128)} %order_ref.1, ...), custom_call_target="tpu_custom_call" | custom-call | tf_op jit(solution)/shard_map/pallas_call | solution.py:293
  85.8 0.0 copy-start.1
  85.8 0.0 copy-start.2
  85.9 2.4 %copy.17 = bf16[256,2048]{1,0:T(8,128)(2,1)} copy(bf16[256,2048]{1,0:T(8,128)(2,1)} %get-tuple-element.8) | data formatting | bytes 2097152
  88.3 0.0 copy-done.1
  88.3 0.0 copy-start
  88.3 1.1 %copy.18 = bf16[256,3072]{1,0:T(8,128)(2,1)} copy(bf16[256,3072]{1,0:T(8,128)(2,1)S(1)} %copy-done.1) | data formatting | bytes 3145728
  89.4 0.0 copy-done.2
  89.4 0.6 copy.19
  90.1 0.4 copy-done
  90.5 1.3 %copy.20 = f32[128,4096]{1,0:T(8,128)} copy(f32[128,4096]{1,0:T(8,128)S(1)} %copy-done) | data formatting | bytes 4194304
Async XLA Ops:
  85.8 2.4 %copy-start.1 = (bf16[256,3072]{1,0:T(8,128)(2,1)S(1)}, bf16[256,3072]{1,0:T(8,128)(2,1)}, u32[]{:S(2)}) copy-start(bf16[256,3072]{1,0:T(8,128)(2,1)} %get-tuple-element.9) | copy-start | bytes 4718596
  85.8 3.6 %copy-start.2 = (f32[32,576]{1,0:T(8,128)S(1)}, f32[32,576]{1,0:T(8,128)}, u32[]{:S(2)}) copy-start(f32[32,576]{1,0:T(8,128)} %get-tuple-element.10) | copy-start | bytes 221188
  88.3 2.2 %copy-start = (f32[128,4096]{1,0:T(8,128)S(1)}, f32[128,4096]{1,0:T(8,128)}, u32[]{:S(2)}) copy-start(f32[128,4096]{1,0:T(8,128)} %get-tuple-element.11) | copy-start | bytes 6291460

commit v3 on v2

--- a/solution.py
+++ b/solution.py
@@ -14,6 +14,7 @@
 ROPE = QK - NOPE
 GROUP = 128
 HIDDEN = -1e30
+LOG2_E = 1.4426950408889634
 
 
 def dot(a, b):
@@ -43,39 +44,57 @@
     lax.fori_loop(0, n_slots, slot, 0)
 
 
-def head_pair(pair, rope, q_ref, kv, dout, attn_ref, qg_ref, rope_acc, bias):
+def head_pair(pair, rope, q_ref, kv, dkv, dout, attn_ref, qg_ref, rope_acc, bias):
     scale = QK**-0.5
-    q_at = pl.multiple_of(pair * (2 * QK), 2 * QK)
-    o_at = pl.multiple_of(pair * (2 * VDIM), 2 * VDIM)
-    query_pair = q_ref[:, pl.ds(q_at, 2 * QK)]
-    query_grads = []
-    rope_sum = None
+    q_at = pl.ds(pl.multiple_of(pair * (2 * QK), 2 * QK), 2 * QK)
+    query_pair = q_ref[:, q_at]
+    v_at = [pl.ds(pl.multiple_of(pair * 256 + j * VDIM, VDIM), VDIM) for j in range(2)]
+    query = [query_pair[:, j * QK : (j + 1) * QK] for j in range(2)]
+    grad = [dout[:, v_at[j]] for j in range(2)]
+
+    def key(j):
+        return jnp.concatenate([kv[:, j * 256 : j * 256 + NOPE], rope], axis=1)
+
+    def value(j):
+        return kv[:, j * 256 + NOPE : (j + 1) * 256]
+
+    def softmax(score):
+        top = jnp.max(score, axis=0, keepdims=True)
+        weight = jnp.exp2((score - top) * (scale * LOG2_E))
+        return weight * (1.0 / jnp.sum(weight, axis=0, keepdims=True))
+
+    def value_side(j, prob_low):
+        dprob = dot_last(value(j), grad[j])
+        out_t = dot(value(j).T, prob_low)
+        delta = jnp.sum(grad[j].astype(jnp.float32).T * out_t, axis=0, keepdims=True)
+        attn_ref[:, v_at[j]] = out_t.T.astype(jnp.bfloat16)
+        return dprob, delta
+
+    def key_side(j, dscore, prob_low):
+        dkey = dot(dscore, query[j])
+        dvalue = dot(prob_low, grad[j])
+        query_grad = dot(key(j).T, dscore).T
+        at = pl.multiple_of(pair * 512 + j * 256, 256)
+        dkv[:, pl.ds(at, NOPE)] = dkey[:, :NOPE].astype(jnp.bfloat16)
+        dkv[:, pl.ds(at + NOPE, VDIM)] = dvalue.astype(jnp.bfloat16)
+        return dkey[:, NOPE:], query_grad
+
+    score = [dot_last(key(j), query[j]) + bias[...] for j in range(2)]
+    prob, low, dprob, delta = [], [], [], []
     for j in range(2):
-        kv_at = pl.multiple_of(pair * 512 + j * 256, 256)
-        v_at = pl.multiple_of(pair * 256 + j * VDIM, VDIM)
-        key = jnp.concatenate([kv[:, pl.ds(kv_at, NOPE)], rope], axis=1)
-        value = kv[:, pl.ds(kv_at + NOPE, VDIM)]
-        query = query_pair[:, j * QK : (j + 1) * QK]
-        grad = dout[:, pl.ds(v_at, VDIM)]
-        score = dot_last(key, query) + bias[...]
-        top = jnp.max(score, axis=0, keepdims=True)
-        weight = jnp.exp((score - top) * scale)
-        prob = weight * (1.0 / jnp.sum(weight, axis=0, keepdims=True))
-        prob_low = prob.astype(jnp.bfloat16)
-        out_t = dot(value.T, prob_low)
-        delta = jnp.sum(grad.astype(jnp.float32).T * out_t, axis=0, keepdims=True)
-        attn_ref[:, pl.ds(v_at, VDIM)] = out_t.T.astype(jnp.bfloat16)
-        dprob = dot_last(value, grad)
-        dscore = (prob * (dprob - delta) * scale).astype(jnp.bfloat16)
-        query_grads.append(dot(key.T, dscore).T)
-        dkey = dot(dscore, query)
-        dvalue = dot(prob_low, grad)
-        kv[:, pl.ds(kv_at, NOPE)] = dkey[:, :NOPE].astype(jnp.bfloat16)
-        kv[:, pl.ds(kv_at + NOPE, VDIM)] = dvalue.astype(jnp.bfloat16)
-        part = dkey[:, NOPE:]
-        rope_sum = part if rope_sum is None else rope_sum + part
-    qg_ref[:, pl.ds(q_at, 2 * QK)] = jnp.concatenate(query_grads, axis=1).astype(jnp.bfloat16)
-    rope_acc[...] += rope_sum
+        prob.append(softmax(score[j]))
+        low.append(prob[j].astype(jnp.bfloat16))
+        grads, rest = value_side(j, low[j])
+        dprob.append(grads)
+        delta.append(rest)
+    rope_grads, query_grads = [], []
+    for j in range(2):
+        dscore = (prob[j] * (dprob[j] - delta[j]) * scale).astype(jnp.bfloat16)
+        rope_grad, query_grad = key_side(j, dscore, low[j])
+        rope_grads.append(rope_grad)
+        query_grads.append(query_grad)
+    qg_ref[:, q_at] = jnp.concatenate(query_grads, axis=1).astype(jnp.bfloat16)
+    rope_acc[...] += rope_grads[0] + rope_grads[1]
 
 
 def remote(src, dst, send_sem, recv_sem, ctx, head):
@@ -93,16 +112,16 @@
     n_ctx, n_head,
     lat_ref, lr_ref, sl_ref, tl_ref, order_ref, q_hbm, w_hbm, g_hbm,
     attn_ref, qg_ref, lg_ref, wg_ref,
-    lat, q_ref, w_ref, g_ref, kv, dout, bias, lat_t, rope_acc,
-    wt, wt_in, terms, core_in, comb, ctx_in, zsum, z_in,
+    lat, q_ref, w_ref, g_ref, kv, dkv, dout, bias, lat_t, rope_acc,
+    wt, a_in, a_sum, a_in2, b_in, b_sum, b_in2, terms, core_in, comb, ctx_in, zsum, z_in,
     load_sem, lat_send, lat_recv, fwd_send, fwd_recv, wt_send, wt_recv,
     core_send, core_recv, ctx_send, ctx_recv, z_send, z_recv,
 ):
-    rows, keys = lat_ref.shape[0], lat.shape[0]
+    rows, keys = lat_ref.shape[1], lat.shape[0]
     n_pairs = q_ref.shape[1] // (2 * QK)
     n_z = n_head // 2
+    n_minor = n_ctx // 2
     half = rows // 2
-    own_rows = KV_RANK // n_ctx
     f32, bf16 = jnp.float32, jnp.bfloat16
     me, head = lax.axis_index("ctx"), lax.axis_index("head")
     core, z = head % 2, head // 2
@@ -124,6 +143,7 @@
     def z_peer(d):
         return (z + d) % n_z
 
+    lat[pl.ds(pl.multiple_of(me * rows, rows), rows), :] = lat_ref[...].T
     barrier = pltpu.get_barrier_semaphore()
     peers = [(ctx_peer(d), head) for d in range(1, n_ctx)]
     peers += [(me, z_peer(d) * 2 + core) for d in range(1, n_z)]
@@ -136,10 +156,8 @@
         return lat.at[pl.ds(pl.multiple_of(block * rows + part * half, half), half), :]
 
     def lat_copy(d, to, block, part):
-        return remote(
-            lat_ref.at[pl.ds(pl.multiple_of(core * half, half), half), :],
-            lat_rows(block, part), lat_send.at[d - 1], lat_recv.at[d - 1], to, head,
-        )
+        place = lat_rows(block, part)
+        return remote(place, place, lat_send.at[d - 1], lat_recv.at[d - 1], to, head)
 
     def fwd_copy(d, part):
         place = lat_rows(ctx_source(d), part)
@@ -148,7 +166,6 @@
     order = [2, 1, 3] if n_ctx == 4 else list(range(1, n_ctx))
     for d in order:
         lat_copy(d, ctx_peer(d), me, core).start()
-    lat[pl.ds(pl.multiple_of(me * rows, rows), rows), :] = lat_ref[...]
 
     fill_bias(order_ref, bias, rows, keys // GROUP)
     tok_weight = jnp.clip(jnp.exp(lr_ref[...]), 0.8, 1.25) * (tl_ref[...] - sl_ref[...])
@@ -173,20 +190,69 @@
     loads[1].wait()
     loads[2].wait()
 
-    def wt_copy(d, pair):
-        to = ctx_peer(d)
-        return remote(
-            wt.at[pair, pl.ds(pl.multiple_of(to * own_rows, own_rows), own_rows), :],
-            wt_in.at[d - 1, pair], wt_send.at[d - 1, pair], wt_recv.at[d - 1, pair], to, head,
-        )
+    u, v = me // n_minor, me % n_minor
+    u_peer = 1 - u
+
+    def v_peer(d):
+        return (v + d) % n_minor
+
+    def minor_first(d, pair):
+        return remote(
+            wt.at[pair, 0, :, v_peer(d)], a_in.at[d - 1, pair],
+            wt_send.at[d - 1, pair], wt_recv.at[d - 1, pair], u * n_minor + v_peer(d), head,
+        )
+
+    def major_first(pair):
+        return remote(
+            wt.at[pair, 1, u_peer], b_in.at[pair],
+            wt_send.at[n_minor - 1, pair], wt_recv.at[n_minor - 1, pair],
+            u_peer * n_minor + v, head,
+        )
+
+    def major_second(pair):
+        return remote(
+            a_sum.at[pair], a_in2.at[pair],
+            wt_send.at[n_minor, pair], wt_recv.at[n_minor, pair], u_peer * n_minor + v, head,
+        )
+
+    def minor_second(d, pair):
+        return remote(
+            b_sum.at[d - 1, pair], b_in2.at[d - 1, pair],
+            wt_send.at[n_minor + d, pair], wt_recv.at[n_minor + d, pair],
+            u * n_minor + v_peer(d), head,
+        )
+
+    def pass_on(pair):
+        total = wt[pair, 0, u_peer, v].astype(f32)
+        for d in range(1, n_minor):
+            minor_first(d, pair).wait_recv()
+            total += a_in[d - 1, pair, u_peer].astype(f32)
+        a_sum[pair] = total.astype(bf16)
+        major_second(pair).start()
+        major_first(pair).wait_recv()
+        for d in range(1, n_minor):
+            total = wt[pair, 1, u, v_peer(d)].astype(f32) + b_in[pair, v_peer(d)].astype(f32)
+            b_sum[d - 1, pair] = total.astype(bf16)
+            minor_second(d, pair).start()
 
     def pair_step(pair, carry):
-        at = pl.multiple_of(pair * 512, 512)
-        kv[:, pl.ds(at, 512)] = dot(lat[:, :KV_RANK], w_ref[:, pl.ds(at, 512)]).astype(bf16)
-        head_pair(pair, lat[:, KV_RANK:], q_ref, kv, dout, attn_ref, qg_ref, rope_acc, bias)
-        wt[pair] = dot(lat_t[...], kv[:, pl.ds(at, 512)]).astype(bf16)
-        for d in order:
-            wt_copy(d, pair).start()
+        at = pl.ds(pl.multiple_of(pair * 512, 512), 512)
+        kv[...] = dot(lat[:, :KV_RANK], w_ref[:, at]).astype(bf16)
+        head_pair(
+            pair, lat[:, KV_RANK:], q_ref, kv, dkv, dout, attn_ref, qg_ref, rope_acc, bias
+        )
+        term = dot(lat_t[...], dkv[:, at]).astype(bf16)
+        for j in range(2):
+            part = term[:, j * 256 : (j + 1) * 256]
+            wt[pair, j] = part.reshape(wt.shape[2:])
+        for d in range(1, n_minor):
+            minor_first(d, pair).start()
+        major_first(pair).start()
+
+        @pl.when(pair > 0)
+        def _():
+            pass_on(pair - 1)
+
         return carry
 
     lax.fori_loop(0, n_pairs, pair_step, 0)
@@ -215,10 +281,14 @@
     def chunk(i, carry):
         block = (me + 1 + i) % n_ctx
         at = pl.ds(pl.multiple_of(block * rows, rows), rows)
-        main = dot_last(kv[at, :], w_ref[...])
+        main = dot_last(dkv[at, :], w_ref[...])
         whole = jnp.concatenate([main, rope_acc[at, :]], axis=1).astype(bf16)
         terms[block] = whole.reshape(terms.shape[1:])
         core_copy(block).start()
+
+        @pl.when(i == 0)
+        def _():
+            pass_on(n_pairs - 1)
 
         @pl.when(i > 0)
         def _():
@@ -237,13 +307,16 @@
         z_copy(d).start()
 
     def gather_weight(pair, carry):
-        at = pl.ds(pl.multiple_of(pair * 512, 512), 512)
-        mine = pl.ds(pl.multiple_of(me * own_rows, own_rows), own_rows)
-        total = wt[pair, mine, :].astype(f32)
-        for d in order:
-            wt_copy(d, pair).wait_recv()
-            total += wt_in[d - 1, pair].astype(f32)
-        wg_ref[:, at] = total
+        major_second(pair).wait_recv()
+        total = wt[pair, 0, u, v].astype(f32) + a_in2[pair].astype(f32)
+        for d in range(1, n_minor):
+            total += a_in[d - 1, pair, u].astype(f32)
+        wg_ref[:, pl.ds(pl.multiple_of(pair * 512, 512), 256)] = total
+        total = wt[pair, 1, u, v].astype(f32) + b_in[pair, v].astype(f32)
+        for d in range(1, n_minor):
+            minor_second(d, pair).wait_recv()
+            total += b_in2[d - 1, pair].astype(f32)
+        wg_ref[:, pl.ds(pl.multiple_of(pair * 512 + 256, 256), 256)] = total
         return carry
 
     lax.fori_loop(0, n_pairs, gather_weight, 0)
@@ -268,8 +341,11 @@
     lax.fori_loop(0, n_ctx, drain_core, 0)
 
     def drain_weight(pair, carry):
-        for d in order:
-            wt_copy(d, pair).wait_send()
+        for d in range(1, n_minor):
+            minor_first(d, pair).wait_send()
+            minor_second(d, pair).wait_send()
+        major_first(pair).wait_send()
+        major_second(pair).wait_send()
         return carry
 
     lax.fori_loop(0, n_pairs, drain_weight, 0)
@@ -283,6 +359,7 @@
     keys = rows * n_ctx
     n_z, per = n_head // 2, rows // n_head
     n_pairs = queries.shape[1] // (2 * QK)
+    n_minor = n_ctx // 2
     own_rows = KV_RANK // n_ctx
     vmem = pl.BlockSpec(memory_space=pltpu.VMEM)
     smem = pl.BlockSpec(memory_space=pltpu.SMEM)
@@ -305,13 +382,19 @@
             pltpu.VMEM(queries.shape, bf16),
             pltpu.VMEM(up_weight.shape, bf16),
             pltpu.VMEM(out_grad.shape, bf16),
+            pltpu.VMEM((keys, 512), bf16),
             pltpu.VMEM((keys, up_weight.shape[1]), bf16),
             pltpu.VMEM(out_grad.shape, bf16),
             pltpu.VMEM((keys, rows), f32),
             pltpu.VMEM((KV_RANK, keys), bf16),
             pltpu.VMEM((keys, ROPE), f32),
-            pltpu.VMEM((n_pairs, KV_RANK, 512), bf16),
-            pltpu.VMEM((n_ctx - 1, n_pairs, own_rows, 512), bf16),
+            pltpu.VMEM((n_pairs, 2, 2, n_minor, own_rows, 256), bf16),
+            pltpu.VMEM((n_minor - 1, n_pairs, 2, own_rows, 256), bf16),
+            pltpu.VMEM((n_pairs, own_rows, 256), bf16),
+            pltpu.VMEM((n_pairs, own_rows, 256), bf16),
+            pltpu.VMEM((n_pairs, n_minor, own_rows, 256), bf16),
+            pltpu.VMEM((n_minor - 1, n_pairs, own_rows, 256), bf16),
+            pltpu.VMEM((n_minor - 1, n_pairs, own_rows, 256), bf16),
             pltpu.VMEM((n_ctx, n_z, 2, per, width), bf16),
             pltpu.VMEM((n_ctx, n_z, per, width), bf16),
             pltpu.VMEM((n_ctx, n_z, per, width), bf16),
@@ -323,8 +406,8 @@
             dma((n_ctx - 1,)),
             dma((n_ctx - 1,)),
             dma((n_ctx - 1,)),
-            dma((n_ctx - 1, n_pairs)),
-            dma((n_ctx - 1, n_pairs)),
+            dma((2 * n_minor, n_pairs)),
+            dma((2 * n_minor, n_pairs)),
             dma((n_ctx,)),
             dma((n_ctx,)),
             dma((n_ctx - 1,)),
@@ -336,7 +419,7 @@
             vmem_limit_bytes=60 * 2**20, collective_id=0, has_side_effects=True
         ),
     )(
-        latent,
+        latent.T,
         logratio.reshape(1, rows),
         student_logprob.reshape(1, rows),
         teacher_logprob.reshape(1, rows),

time: 92 us -> 80.1 us (0.87)
  Pallas kernels: 83.3 us -> 73.3 us
  local copies, waits for them, and re-layouts: 7.8 us -> 5.94 us
    pallas_call x1, Pallas kernels: 83.3 us -> 73.3 us  [local(): pl.pallas_call(functools.partial(kernel, n_ctx, n_head), out_shape=(shape...]
    unnamed x11 -> x10, local copies, waits for them, and re-layouts: 7.8 us -> 5.94 us
where the time goes in v3:
time: 80.1 us; the launch traced here: 79.9 us
  Pallas kernels  73.3 us (92%)
  local copies, waits for them, and re-layouts  5.94 us (7%)
    pallas_call x1, Pallas kernels, local(): pl.pallas_call(functools.partial(kernel, n_ctx, n_head), out_shape=(shape...  73.3 us
    unnamed x10, local copies, waits for them, and re-layouts  5.94 us

profile of v3, /device:TPU:0, one launch (start us, length us, event | category | flops | bytes accessed | tf_op | source)
XLA Modules:
  0.0 79.9 jit_solution(12381746779355054465)
XLA Ops:
  0.6 73.3 %shard_map.111 = (bf16[256,2048]{1,0:T(8,128)(2,1)}, bf16[256,3072]{1,0:T(8,128)(2,1)}, f32[32,576]{1,0:T(8,128)}, f32[128,4096]{1,0:T(8,128)}) custom-call(bf16[576,256]{1,0:T(8,128)(2,1)} %bitcast.4, f32[1,256]{1,0:T(1,128)} %bitcast.5, f32[1,256]{1,0:T(1,128)} %bitcast.6, f32[1,256]{1,0:T(1,128)} %bitcast.7, s32[8]{0:T(128)} %order_ref.1, ...), custom_call_target="tpu_custom_call" | custom-call | tf_op jit(solution)/shard_map/pallas_call | solution.py:370
  74.0 0.0 copy-start.1
  74.0 0.0 copy-start.2
  74.0 2.4 %copy.16 = bf16[256,2048]{1,0:T(8,128)(2,1)} copy(bf16[256,2048]{1,0:T(8,128)(2,1)} %get-tuple-element.8) | data formatting | bytes 2097152
  76.4 0.0 copy-done.1
  76.4 0.0 copy-start
  76.4 1.1 %copy.17 = bf16[256,3072]{1,0:T(8,128)(2,1)} copy(bf16[256,3072]{1,0:T(8,128)(2,1)S(1)} %copy-done.1) | data formatting | bytes 3145728
  77.6 0.0 copy-done.2
  77.6 0.6 copy.18
  78.2 0.4 copy-done
  78.6 1.3 %copy.19 = f32[128,4096]{1,0:T(8,128)} copy(f32[128,4096]{1,0:T(8,128)S(1)} %copy-done) | data formatting | bytes 4194304
Async XLA Ops:
  74.0 2.4 %copy-start.1 = (bf16[256,3072]{1,0:T(8,128)(2,1)S(1)}, bf16[256,3072]{1,0:T(8,128)(2,1)}, u32[]{:S(2)}) copy-start(bf16[256,3072]{1,0:T(8,128)(2,1)} %get-tuple-element.9) | copy-start | bytes 4718596
  74.0 3.6 %copy-start.2 = (f32[32,576]{1,0:T(8,128)S(1)}, f32[32,576]{1,0:T(8,128)}, u32[]{:S(2)}) copy-start(f32[32,576]{1,0:T(8,128)} %get-tuple-element.10) | copy-start | bytes 221188
  76.4 2.2 %copy-start = (f32[128,4096]{1,0:T(8,128)S(1)}, f32[128,4096]{1,0:T(8,128)}, u32[]{:S(2)}) copy-start(f32[128,4096]{1,0:T(8,128)} %get-tuple-element.11) | copy-start | bytes 6291460

commit v4 on v3

--- a/solution.py
+++ b/solution.py
@@ -53,10 +53,11 @@
     grad = [dout[:, v_at[j]] for j in range(2)]
 
     def key(j):
-        return jnp.concatenate([kv[:, j * 256 : j * 256 + NOPE], rope], axis=1)
+        at = pl.ds(pl.multiple_of(pair * 512 + j * 256, 256), NOPE)
+        return jnp.concatenate([kv[:, at], rope], axis=1)
 
     def value(j):
-        return kv[:, j * 256 + NOPE : (j + 1) * 256]
+        return kv[:, pl.ds(pl.multiple_of(pair * 512 + j * 256 + NOPE, VDIM), VDIM)]
 
     def softmax(score):
         top = jnp.max(score, axis=0, keepdims=True)
@@ -181,13 +182,33 @@
 
     lax.fori_loop(0, n_pairs, weigh, 0)
 
-    for d in order:
+    def up_project(block):
+        at = pl.ds(pl.multiple_of(block * rows, rows), rows)
+        lat_t[:, at] = lat[at, :KV_RANK].T
+
+        def columns(pair, carry):
+            cols = pl.ds(pl.multiple_of(pair * 512, 512), 512)
+            kv[at, cols] = dot(lat[at, :KV_RANK], w_ref[:, cols]).astype(bf16)
+            return carry
+
+        lax.fori_loop(0, n_pairs, columns, 0)
+
+    def arrive(d):
         lat_copy(d, ctx_peer(d), ctx_source(d), core).wait_recv()
         fwd_copy(d, core).start()
-    for d in order:
+
+    def use(d):
         fwd_copy(d, 1 - core).wait_recv()
-    lat_t[...] = lat[:, :KV_RANK].T
+        up_project(ctx_source(d))
+
     loads[1].wait()
+    up_project(me)
+    arrive(order[0])
+    use(order[0])
+    for d in order[1:]:
+        arrive(d)
+    for d in order[1:]:
+        use(d)
     loads[2].wait()
 
     u, v = me // n_minor, me % n_minor
@@ -237,7 +258,6 @@
 
     def pair_step(pair, carry):
         at = pl.ds(pl.multiple_of(pair * 512, 512), 512)
-        kv[...] = dot(lat[:, :KV_RANK], w_ref[:, at]).astype(bf16)
         head_pair(
             pair, lat[:, KV_RANK:], q_ref, kv, dkv, dout, attn_ref, qg_ref, rope_acc, bias
         )
@@ -349,6 +369,15 @@
         return carry
 
     lax.fori_loop(0, n_pairs, drain_weight, 0)
+
+
+def write_out(*refs):
+    sem = refs[8]
+    copies = [pltpu.make_async_copy(refs[i], refs[4 + i], sem.at[i]) for i in range(4)]
+    for copy in copies:
+        copy.start()
+    for copy in copies:
+        copy.wait()
 
 
 def local(
@@ -367,13 +396,13 @@
     bf16, f32 = jnp.bfloat16, jnp.float32
     dma = pltpu.SemaphoreType.DMA
     shape = jax.ShapeDtypeStruct
-    return pl.pallas_call(
+    results = pl.pallas_call(
         functools.partial(kernel, n_ctx, n_head),
         out_shape=(
-            shape(out_grad.shape, bf16),
-            shape(queries.shape, bf16),
-            shape((per, width), f32),
-            shape((own_rows, up_weight.shape[1]), f32),
+            pltpu.VMEM(out_grad.shape, bf16),
+            pltpu.VMEM(queries.shape, bf16),
+            pltpu.VMEM((per, width), f32),
+            pltpu.VMEM((own_rows, up_weight.shape[1]), f32),
         ),
         in_specs=[vmem] * 4 + [smem] + [anywhere] * 3,
         out_specs=[vmem] * 4,
@@ -382,7 +411,7 @@
             pltpu.VMEM(queries.shape, bf16),
             pltpu.VMEM(up_weight.shape, bf16),
             pltpu.VMEM(out_grad.shape, bf16),
-            pltpu.VMEM((keys, 512), bf16),
+            pltpu.VMEM((keys, up_weight.shape[1]), bf16),
             pltpu.VMEM((keys, up_weight.shape[1]), bf16),
             pltpu.VMEM(out_grad.shape, bf16),
             pltpu.VMEM((keys, rows), f32),
@@ -416,7 +445,7 @@
             dma((n_z - 1,)),
         ],
         compiler_params=pltpu.CompilerParams(
-            vmem_limit_bytes=60 * 2**20, collective_id=0, has_side_effects=True
+            vmem_limit_bytes=58 * 2**20, collective_id=0, has_side_effects=True
         ),
     )(
         latent.T,
@@ -428,6 +457,13 @@
         up_weight,
         out_grad,
     )
+    return pl.pallas_call(
+        write_out,
+        out_shape=tuple(shape(result.shape, result.dtype) for result in results),
+        in_specs=[anywhere] * 4,
+        out_specs=[anywhere] * 4,
+        scratch_shapes=[dma((4,))],
+    )(*results)
 
 
 def solution(mesh):

time: 80.1 us -> 229 us (2.86)
  Pallas kernels: 73.3 us -> 224 us
    pallas_call x1 -> x2, Pallas kernels: 73.3 us -> 224 us  [the longest x1 147 us: local(): pl.pallas_call(write_out, out_shape=tuple((shape(result.shape, result.dty...]
    unnamed x10 -> x8, local copies, waits for them, and re-layouts: 5.94 us -> 4.07 us
where the time goes in v4:
time: 229 us
  Pallas kernels  224 us (98%)
  local copies, waits for them, and re-layouts  4.07 us (2%)
    pallas_call x1, Pallas kernels, local(): pl.pallas_call(write_out, out_shape=tuple((shape(result.shape, result.dty...  147 us
    pallas_call x1, Pallas kernels, local(): pl.pallas_call(functools.partial(kernel, n_ctx, n_head), out_shape=(pltpu...  77.7 us

profile of v4, /device:TPU:0, one launch (start us, length us, event | category | flops | bytes accessed | tf_op | source)
XLA Modules:
  0.0 229.0 jit_solution(14961534866264024529)
XLA Ops:
  0.6 77.7 %shard_map.111 = (bf16[256,2048]{1,0:T(8,128)(2,1)S(1)}, bf16[256,3072]{1,0:T(8,128)(2,1)S(1)}, f32[32,576]{1,0:T(8,128)S(1)}, f32[128,4096]{1,0:T(8,128)S(1)}) custom-call(bf16[576,256]{1,0:T(8,128)(2,1)} %bitcast.4, f32[1,256]{1,0:T(1,128)} %bitcast.5, f32[1,256]{1,0:T(1,128)} %bitcast.6, f32[1,256]{1,0:T(1,128)} %bitcast.7, s32[8]{0:T(128)} %order_ref.1, ...), custom_call_target="tpu_custom_call" | custom-call | tf_op jit(solution)/shard_map/pallas_call | solution.py:399
  78.4 0.0 copy-start
  78.4 1.3 copy-done
  79.7 0.0 copy-start.1
  79.7 1.1 copy-done.1
  80.8 0.0 copy-start.2
  80.9 1.0 copy-done.2
  81.8 0.0 copy-start.3
  81.8 0.6 copy-done.3
  82.5 146.6 %shard_map.112 = (bf16[256,2048]{1,0:T(8,128)(2,1)}, bf16[256,3072]{1,0:T(8,128)(2,1)}, f32[32,576]{1,0:T(8,128)}, f32[128,4096]{1,0:T(8,128)}) custom-call(bf16[256,2048]{1,0:T(8,128)(2,1)} %copy-done.2, bf16[256,3072]{1,0:T(8,128)(2,1)} %copy-done.1, f32[32,576]{1,0:T(8,128)} %copy-done.3, f32[128,4096]{1,0:T(8,128)} %copy-done), custom_call_target="tpu_custom_call" | custom-call | tf_op jit(solution)/shard_map/pallas_call | solution.py:460
Async XLA Ops:
  78.4 1.3 copy-start
  79.7 1.1 copy-start.1
  80.8 1.0 copy-start.2
  81.8 0.6 copy-start.3

commit v5 on v3

--- a/solution.py
+++ b/solution.py
@@ -11,7 +11,6 @@
 VDIM = 128
 KV_RANK = 512
 QK = 192
-ROPE = QK - NOPE
 GROUP = 128
 HIDDEN = -1e30
 LOG2_E = 1.4426950408889634
@@ -44,7 +43,7 @@
     lax.fori_loop(0, n_slots, slot, 0)
 
 
-def head_pair(pair, rope, q_ref, kv, dkv, dout, attn_ref, qg_ref, rope_acc, bias):
+def head_pair(pair, rope, q_ref, kv, dkv, dout, attn_ref, qg_ref, acc, bias):
     scale = QK**-0.5
     q_at = pl.ds(pl.multiple_of(pair * (2 * QK), 2 * QK), 2 * QK)
     query_pair = q_ref[:, q_at]
@@ -74,9 +73,8 @@
         dkey = dot(dscore, query[j])
         dvalue = dot(prob_low, grad[j])
         query_grad = dot(key(j).T, dscore).T
-        at = pl.multiple_of(pair * 512 + j * 256, 256)
-        dkv[:, pl.ds(at, NOPE)] = dkey[:, :NOPE].astype(jnp.bfloat16)
-        dkv[:, pl.ds(at + NOPE, VDIM)] = dvalue.astype(jnp.bfloat16)
+        dkv[:, j * 256 : j * 256 + NOPE] = dkey[:, :NOPE].astype(jnp.bfloat16)
+        dkv[:, j * 256 + NOPE : (j + 1) * 256] = dvalue.astype(jnp.bfloat16)
         return dkey[:, NOPE:], query_grad
 
     score = [dot_last(key(j), query[j]) + bias[...] for j in range(2)]
@@ -94,7 +92,7 @@
         rope_grads.append(rope_grad)
         query_grads.append(query_grad)
     qg_ref[:, q_at] = jnp.concatenate(query_grads, axis=1).astype(jnp.bfloat16)
-    rope_acc[...] += rope_grads[0] + rope_grads[1]
+    acc[:, KV_RANK:] += rope_grads[0] + rope_grads[1]
 
 
 def remote(src, dst, send_sem, recv_sem, ctx, head):
@@ -112,7 +110,7 @@
     n_ctx, n_head,
     lat_ref, lr_ref, sl_ref, tl_ref, order_ref, q_hbm, w_hbm, g_hbm,
     attn_ref, qg_ref, lg_ref, wg_ref,
-    lat, q_ref, w_ref, g_ref, kv, dkv, dout, bias, lat_t, rope_acc,
+    lat, q_ref, w_ref, g_ref, kv, dkv, dout, bias, lat_t, acc,
     wt, a_in, a_sum, a_in2, b_in, b_sum, b_in2, terms, core_in, comb, ctx_in, zsum, z_in,
     load_sem, lat_send, lat_recv, fwd_send, fwd_recv, wt_send, wt_recv,
     core_send, core_recv, ctx_send, ctx_recv, z_send, z_recv,
@@ -171,7 +169,7 @@
     tok_weight = jnp.clip(jnp.exp(lr_ref[...]), 0.8, 1.25) * (tl_ref[...] - sl_ref[...])
     tok_weight = jnp.broadcast_to(tok_weight, (128, rows)).T
     two = jnp.concatenate([tok_weight, tok_weight], axis=1)
-    rope_acc[...] = jnp.zeros_like(rope_acc)
+    acc[...] = jnp.zeros_like(acc)
     loads[0].wait()
 
     def weigh(pair, carry):
@@ -239,9 +237,10 @@
         at = pl.ds(pl.multiple_of(pair * 512, 512), 512)
         kv[...] = dot(lat[:, :KV_RANK], w_ref[:, at]).astype(bf16)
         head_pair(
-            pair, lat[:, KV_RANK:], q_ref, kv, dkv, dout, attn_ref, qg_ref, rope_acc, bias
-        )
-        term = dot(lat_t[...], dkv[:, at]).astype(bf16)
+            pair, lat[:, KV_RANK:], q_ref, kv, dkv, dout, attn_ref, qg_ref, acc, bias
+        )
+        acc[:, :KV_RANK] += dot_last(dkv[...], w_ref[:, at])
+        term = dot(lat_t[...], dkv[...]).astype(bf16)
         for j in range(2):
             part = term[:, j * 256 : (j + 1) * 256]
             wt[pair, j] = part.reshape(wt.shape[2:])
@@ -249,9 +248,9 @@
             minor_first(d, pair).start()
         major_first(pair).start()
 
-        @pl.when(pair > 0)
+        @pl.when(pair > 1)
         def _():
-            pass_on(pair - 1)
+            pass_on(pair - 2)
 
         return carry
 
@@ -278,26 +277,23 @@
         core_copy(block).wait_recv()
         return terms[block, :, core].astype(f32) + core_in[block].astype(f32)
 
-    def chunk(i, carry):
+    def to_partner(i, carry):
         block = (me + 1 + i) % n_ctx
         at = pl.ds(pl.multiple_of(block * rows, rows), rows)
-        main = dot_last(dkv[at, :], w_ref[...])
-        whole = jnp.concatenate([main, rope_acc[at, :]], axis=1).astype(bf16)
-        terms[block] = whole.reshape(terms.shape[1:])
+        terms[block] = acc[at, :].astype(bf16).reshape(terms.shape[1:])
         core_copy(block).start()
-
-        @pl.when(i == 0)
-        def _():
-            pass_on(n_pairs - 1)
-
-        @pl.when(i > 0)
-        def _():
-            comb[i] = merged((me + i) % n_ctx).astype(bf16)
-            ctx_copy(i).start()
-
-        return carry
-
-    lax.fori_loop(0, n_ctx, chunk, 0)
+        return carry
+
+    def to_owner(d, carry):
+        comb[d] = merged((me + d) % n_ctx).astype(bf16)
+        ctx_copy(d).start()
+        return carry
+
+    lax.fori_loop(0, n_ctx, to_partner, 0)
+    if n_pairs > 1:
+        pass_on(n_pairs - 2)
+    lax.fori_loop(1, n_ctx, to_owner, 0)
+    pass_on(n_pairs - 1)
     total = merged(me)
     for d in order:
         ctx_copy(d).wait_recv()
@@ -366,14 +362,13 @@
     anywhere = pl.BlockSpec(memory_space=pl.ANY)
     bf16, f32 = jnp.bfloat16, jnp.float32
     dma = pltpu.SemaphoreType.DMA
-    shape = jax.ShapeDtypeStruct
     return pl.pallas_call(
         functools.partial(kernel, n_ctx, n_head),
         out_shape=(
-            shape(out_grad.shape, bf16),
-            shape(queries.shape, bf16),
-            shape((per, width), f32),
-            shape((own_rows, up_weight.shape[1]), f32),
+            pltpu.VMEM(out_grad.shape, bf16),
+            pltpu.VMEM(queries.shape, bf16),
+            pltpu.VMEM((per, width), f32),
+            pltpu.VMEM((own_rows, up_weight.shape[1]), f32),
         ),
         in_specs=[vmem] * 4 + [smem] + [anywhere] * 3,
         out_specs=[vmem] * 4,
@@ -383,11 +378,11 @@
             pltpu.VMEM(up_weight.shape, bf16),
             pltpu.VMEM(out_grad.shape, bf16),
             pltpu.VMEM((keys, 512), bf16),
-            pltpu.VMEM((keys, up_weight.shape[1]), bf16),
+            pltpu.VMEM((keys, 512), bf16),
             pltpu.VMEM(out_grad.shape, bf16),
             pltpu.VMEM((keys, rows), f32),
             pltpu.VMEM((KV_RANK, keys), bf16),
-            pltpu.VMEM((keys, ROPE), f32),
+            pltpu.VMEM((keys, width), f32),
             pltpu.VMEM((n_pairs, 2, 2, n_minor, own_rows, 256), bf16),
             pltpu.VMEM((n_minor - 1, n_pairs, 2, own_rows, 256), bf16),
             pltpu.VMEM((n_pairs, own_rows, 256), bf16),
@@ -416,7 +411,7 @@
             dma((n_z - 1,)),
         ],
         compiler_params=pltpu.CompilerParams(
-            vmem_limit_bytes=60 * 2**20, collective_id=0, has_side_effects=True
+            vmem_limit_bytes=58 * 2**20, collective_id=0, has_side_effects=True
         ),
     )(
         latent.T,

time: 80.1 us -> 75.8 us (0.946)
  Pallas kernels: 73.3 us -> 70.9 us
  local copies, waits for them, and re-layouts: 5.94 us -> 4.07 us
    pallas_call x1, Pallas kernels: 73.3 us -> 70.9 us  [local(): pl.pallas_call(functools.partial(kernel, n_ctx, n_head), out_shape=(pltpu...]
    unnamed x10 -> x4, local copies, waits for them, and re-layouts: 5.94 us -> 4.07 us
where the time goes in v5:
time: 75.8 us; the launch traced here: 75.6 us
  Pallas kernels  70.9 us (94%)
  local copies, waits for them, and re-layouts  4.07 us (5%)
    pallas_call x1, Pallas kernels, local(): pl.pallas_call(functools.partial(kernel, n_ctx, n_head), out_shape=(pltpu...  70.9 us
    unnamed x4, local copies, waits for them, and re-layouts  4.07 us

profile of v5, /device:TPU:0, one launch (start us, length us, event | category | flops | bytes accessed | tf_op | source)
XLA Modules:
  0.0 75.6 jit_solution(13845698733598051729)
XLA Ops:
  0.6 70.9 %shard_map.111 = (bf16[256,2048]{1,0:T(8,128)(2,1)S(1)}, bf16[256,3072]{1,0:T(8,128)(2,1)S(1)}, f32[32,576]{1,0:T(8,128)S(1)}, f32[128,4096]{1,0:T(8,128)S(1)}) custom-call(bf16[576,256]{1,0:T(8,128)(2,1)} %bitcast.4, f32[1,256]{1,0:T(1,128)} %bitcast.5, f32[1,256]{1,0:T(1,128)} %bitcast.6, f32[1,256]{1,0:T(1,128)} %bitcast.7, s32[8]{0:T(128)} %order_ref.1, ...), custom_call_target="tpu_custom_call" | custom-call | tf_op jit(solution)/shard_map/pallas_call | solution.py:365
  71.5 1.0 %copy.16 = bf16[256,2048]{1,0:T(8,128)(2,1)} copy(bf16[256,2048]{1,0:T(8,128)(2,1)S(1)} %get-tuple-element.4) | data formatting | bytes 2097152
  72.5 0.6 copy.18
  73.2 1.1 %copy.17 = bf16[256,3072]{1,0:T(8,128)(2,1)} copy(bf16[256,3072]{1,0:T(8,128)(2,1)S(1)} %get-tuple-element.5) | data formatting | bytes 3145728
  74.3 1.3 %copy.19 = f32[128,4096]{1,0:T(8,128)} copy(f32[128,4096]{1,0:T(8,128)S(1)} %get-tuple-element.7) | data formatting | bytes 4194304

commit v6 on v5

--- a/solution.py
+++ b/solution.py
@@ -43,7 +43,7 @@
     lax.fori_loop(0, n_slots, slot, 0)
 
 
-def head_pair(pair, rope, q_ref, kv, dkv, dout, attn_ref, qg_ref, acc, bias):
+def head_pair(pair, rope, q_ref, kv, dkv, dout, attn_ref, qg_ref, acc, bias, beside):
     scale = QK**-0.5
     q_at = pl.ds(pl.multiple_of(pair * (2 * QK), 2 * QK), 2 * QK)
     query_pair = q_ref[:, q_at]
@@ -78,6 +78,7 @@
         return dkey[:, NOPE:], query_grad
 
     score = [dot_last(key(j), query[j]) + bias[...] for j in range(2)]
+    beside()
     prob, low, dprob, delta = [], [], [], []
     for j in range(2):
         prob.append(softmax(score[j]))
@@ -233,20 +234,37 @@
             b_sum[d - 1, pair] = total.astype(bf16)
             minor_second(d, pair).start()
 
-    def pair_step(pair, carry):
+    def latent_terms(pair):
         at = pl.ds(pl.multiple_of(pair * 512, 512), 512)
-        kv[...] = dot(lat[:, :KV_RANK], w_ref[:, at]).astype(bf16)
-        head_pair(
-            pair, lat[:, KV_RANK:], q_ref, kv, dkv, dout, attn_ref, qg_ref, acc, bias
-        )
         acc[:, :KV_RANK] += dot_last(dkv[...], w_ref[:, at])
+
+    def weight_terms(pair):
         term = dot(lat_t[...], dkv[...]).astype(bf16)
         for j in range(2):
             part = term[:, j * 256 : (j + 1) * 256]
             wt[pair, j] = part.reshape(wt.shape[2:])
+
+    def send_weight_terms(pair):
         for d in range(1, n_minor):
             minor_first(d, pair).start()
         major_first(pair).start()
+
+    def pair_step(pair, carry):
+        at = pl.ds(pl.multiple_of(pair * 512, 512), 512)
+        before = (pair + n_pairs - 1) % n_pairs
+        kv[...] = dot(lat[:, :KV_RANK], w_ref[:, at]).astype(bf16)
+
+        def beside():
+            latent_terms(before)
+            weight_terms(before)
+
+        head_pair(
+            pair, lat[:, KV_RANK:], q_ref, kv, dkv, dout, attn_ref, qg_ref, acc, bias, beside
+        )
+
+        @pl.when(pair > 0)
+        def _():
+            send_weight_terms(pair - 1)
 
         @pl.when(pair > 1)
         def _():
@@ -254,6 +272,7 @@
 
         return carry
 
+    dkv[...] = jnp.zeros_like(dkv)
     lax.fori_loop(0, n_pairs, pair_step, 0)
 
     def core_copy(block):
@@ -289,7 +308,10 @@
         ctx_copy(d).start()
         return carry
 
+    latent_terms(n_pairs - 1)
     lax.fori_loop(0, n_ctx, to_partner, 0)
+    weight_terms(n_pairs - 1)
+    send_weight_terms(n_pairs - 1)
     if n_pairs > 1:
         pass_on(n_pairs - 2)
     lax.fori_loop(1, n_ctx, to_owner, 0)

time: 75.8 us -> 78.2 us (1.032)
  Pallas kernels: 70.9 us -> 73.3 us
    pallas_call x1, Pallas kernels: 70.9 us -> 73.3 us  [local(): pl.pallas_call(functools.partial(kernel, n_ctx, n_head), out_shape=(pltpu...]
where the time goes in v6:
time: 78.2 us; the launch traced here: 78 us
  Pallas kernels  73.3 us (94%)
  local copies, waits for them, and re-layouts  4.07 us (5%)
    pallas_call x1, Pallas kernels, local(): pl.pallas_call(functools.partial(kernel, n_ctx, n_head), out_shape=(pltpu...  73.3 us
    unnamed x4, local copies, waits for them, and re-layouts  4.07 us

profile of v6, /device:TPU:0, one launch (start us, length us, event | category | flops | bytes accessed | tf_op | source)
XLA Modules:
  0.0 78.0 jit_solution(7837381042373413962)
XLA Ops:
  0.6 73.3 %shard_map.111 = (bf16[256,2048]{1,0:T(8,128)(2,1)S(1)}, bf16[256,3072]{1,0:T(8,128)(2,1)S(1)}, f32[32,576]{1,0:T(8,128)S(1)}, f32[128,4096]{1,0:T(8,128)S(1)}) custom-call(bf16[576,256]{1,0:T(8,128)(2,1)} %bitcast.4, f32[1,256]{1,0:T(1,128)} %bitcast.5, f32[1,256]{1,0:T(1,128)} %bitcast.6, f32[1,256]{1,0:T(1,128)} %bitcast.7, s32[8]{0:T(128)} %order_ref.1, ...), custom_call_target="tpu_custom_call" | custom-call | tf_op jit(solution)/shard_map/pallas_call | solution.py:387
  74.0 1.0 %copy.16 = bf16[256,2048]{1,0:T(8,128)(2,1)} copy(bf16[256,2048]{1,0:T(8,128)(2,1)S(1)} %get-tuple-element.4) | data formatting | bytes 2097152
  74.9 0.6 copy.18
  75.6 1.1 %copy.17 = bf16[256,3072]{1,0:T(8,128)(2,1)} copy(bf16[256,3072]{1,0:T(8,128)(2,1)S(1)} %get-tuple-element.5) | data formatting | bytes 3145728
  76.7 1.3 %copy.19 = f32[128,4096]{1,0:T(8,128)} copy(f32[128,4096]{1,0:T(8,128)S(1)} %get-tuple-element.7) | data formatting | bytes 4194304
